TPU v7x, 512 devices: a whole 4x4x16 slice. The times are simulated.
512 devices in a mesh: beam: 32 (over x, y, core), freq: 16 (over z).
Axes of the slice: x: 4, y: 4, z: 16, core: 2. Of those that a mesh axis runs over, the one named last changes fastest.
Arguments:
- voltages: bfloat16 [2048, 1024, 256], P(('beam', 'freq')), may hold values from -6 to 6
- gains: float32 [2048, 2, 1024], P(('beam', 'freq')), may hold values from -6 to 6
- channel_map: int32 [2048], P(('beam', 'freq')), may hold values from 0 to 2047, as said below
- positions: float32 [2, 1024], replicated, may hold values from -4 to 4
- directions: float32 [2, 256], replicated, may hold values from -0.5 to 0.5
- local_delay: int32 [256, 128], P('freq'), may hold values from 0 to 16
- merge_table: int32 [3, 480], replicated, may hold values from 0 to 127, as said below
Outputs:
- dedispersed: float32 [256, 256, 128], P('freq', 'beam')
Inputs may be any that keep to these rules, and one draw needn't show every extreme that they name: `channel_map`: stored channels (i * 16 + f) * 4 + l over all i and l hold the sky channels f * 128 to (f + 1) * 128 - 1, each once. `merge_table`: in merge step k (entries 2 * 16 * (2^k - 1) to 2 * 16 * (2^(k+1) - 1) - 1), the two row numbers are below 16 * 2^k and every row number appears; delays run from 0 to 24, each value appearing.
All inputs are finite; a program needn't handle non-finite values.
Results may differ from a plain program's by a relative error of at most 0.005.
Values may be sent and summed in bfloat16 or wider, within the bound.
A program may use at most 128 MiB of HBM per device.

v0:
```python
import functools
import math

import jax
import jax.numpy as jnp
from jax import lax
from jax.experimental import pallas as pl
from jax.experimental.pallas import tpu as pltpu
from jax.sharding import PartitionSpec as P

MESH = pl.DeviceIdType.MESH
F32 = jnp.float32
BF16 = jnp.bfloat16

CHANNELS = 4
ANTENNAS = 1024
BEAMS = 256
SAMPLES = 128
SENDERS = 32
GROUP = 8
GROUPS = SENDERS // GROUP
TURNS = 2
TURN_BEAMS = BEAMS // TURNS
TURN_SENDS = SENDERS // TURNS
OWN_BEAMS = BEAMS // SENDERS
TRIALS = 16
OFFSETS = 17
SUBBANDS = 16
REACH = 2
PLACES = 2 * REACH + 2
NEARS = PLACES - 1
FARS = 2
ENTRIES = 480

SIN_TERMS = (2.22143036, -0.91317465, 0.10983828)
ROUNDER = 12582912.0


def horner(terms, z):
    total = z * terms[-1] + terms[-2]
    for term in terms[-3::-1]:
        total = total * z + term
    return total


def weight_pair(geometry, ratio, gain_re, gain_im):
    turns = geometry * ratio
    rest = turns - ((turns + ROUNDER) - ROUNDER)
    z = rest * rest
    quarter_sin = rest * horner(SIN_TERMS, z)
    square = quarter_sin * quarter_sin
    left = 2.0 - square
    half_sin = quarter_sin * (left * lax.rsqrt(left))
    half_cos = 1.0 - square
    doubled = half_sin + half_sin
    cosine = 1.0 - doubled * half_sin
    sine = doubled * half_cos
    return gain_re * cosine + gain_im * sine, gain_im * cosine - gain_re * sine


def kernel(
    volts_hbm, gains_hbm, channel_hbm, positions_hbm, directions_hbm, delay_hbm, merge_hbm, out_ref,
    gains_ref, channel_ref, positions_ref, directions_ref, delay_ref, merge_ref, volts, geometry, across, intensity, outgoing, incoming, rows_f32, columns,
    selector, partial_f32, window, own_block, window_in, sums_out, sums_in, table_pad, table_vmem, table,
    small_sem, volts_sem, table_sem, send_sem, recv_sem, near_send, near_recv, far_send, far_recv,
):
    beam_at = lax.axis_index("beam")
    freq_at = lax.axis_index("freq")
    row = beam_at // GROUP
    spot = lax.rem(beam_at // 2, GROUPS)
    core = lax.rem(beam_at, 2)
    lean = 1 - 2 * core

    def ring(offset):
        return lax.rem(freq_at + offset + SUBBANDS, SUBBANDS)

    def mate(distance, step, to_core):
        return lax.rem(row + distance, GROUPS) * GROUP + lax.rem(spot + step, GROUPS) * 2 + to_core

    smalls = [
        pltpu.make_async_copy(src, dst, small_sem.at[n])
        for n, (src, dst) in enumerate((
            (merge_hbm, merge_ref), (directions_hbm, directions_ref), (positions_hbm, positions_ref),
            (gains_hbm, gains_ref), (channel_hbm, channel_ref), (delay_hbm, delay_ref),
        ))
    ]
    for small in smalls:
        small.start()
    loads = [
        pltpu.make_async_copy(volts_hbm.at[c], volts.at[c], volts_sem.at[c]) for c in range(CHANNELS)
    ]
    for load in loads:
        load.start()

    barrier = pltpu.get_barrier_semaphore()

    for step in range(1, SENDERS):
        other = lax.rem(beam_at + step, SENDERS)
        pl.semaphore_signal(barrier, inc=1, device_id=(other, freq_at), device_id_type=MESH)
    near_offsets = (-2, 2, -1, 1, 3 * lean)
    far_offsets = (6 * lean, -5 * lean)
    for offset in near_offsets + far_offsets:
        pl.semaphore_signal(barrier, inc=1, device_id=(beam_at, ring(offset)), device_id_type=MESH)

    for small in smalls:
        small.wait()

    for k in range(2):
        across[k] = jnp.transpose(jnp.broadcast_to(directions_ref[k : k + 1, :], (128, BEAMS)))

    def geometry_rows(chip, carry):
        for to_core in range(2):
            at = pl.ds(pl.multiple_of(chip * 16 + to_core * 8, 8), 8)
            to = pl.ds(pl.multiple_of(to_core * (BEAMS // 2) + chip * 8, 8), 8)
            first, second = across[0, at, :], across[1, at, :]
            for n in range(ANTENNAS // 128):
                lanes = pl.ds(n * 128, 128)
                geometry[to, lanes] = (
                    first * positions_ref[0:1, lanes] + second * positions_ref[1:2, lanes]
                )
        return carry

    lax.fori_loop(0, SENDERS // 2, geometry_rows, 0)
    for load in loads:
        load.wait()

    half_width = ANTENNAS // 2

    def beams_of(to_core):
        for c in range(CHANNELS):
            ratio = 1.0 + channel_ref[c].astype(F32) * (1.0 / 2048.0)
            product = None
            for half in range(2):
                lanes = pl.ds(half * half_width, half_width)
                gain_re = jnp.broadcast_to(gains_ref[c, 0:1, lanes] * (1.0 / 32.0), (16, half_width))
                gain_im = jnp.broadcast_to(gains_ref[c, 1:2, lanes] * (1.0 / 32.0), (16, half_width))
                real, imag = [], []
                for n in range(TURN_BEAMS // 16):
                    at = pl.ds(pl.multiple_of(to_core * (BEAMS // 2) + n * 16, 16), 16)
                    pair = weight_pair(geometry[at, lanes], ratio, gain_re, gain_im)
                    real.append(pair[0].astype(BF16))
                    imag.append(pair[1].astype(BF16))
                weights = jnp.concatenate(real + imag, axis=0)
                term = jnp.dot(weights, volts[c, lanes, :], preferred_element_type=F32)
                product = term if product is None else product + term
            beam_re = product[:TURN_BEAMS, :SAMPLES] - product[TURN_BEAMS:, SAMPLES:]
            beam_im = product[:TURN_BEAMS, SAMPLES:] + product[TURN_BEAMS:, :SAMPLES]
            power = beam_re * beam_re + beam_im * beam_im
            mean = jnp.sum(power, axis=1, keepdims=True) * (1.0 / SAMPLES)
            intensity[c] = 0.25 * (power - mean)
        for n in range(TURN_SENDS):
            for pair in range(CHANNELS // 2):
                rows = jnp.concatenate(
                    [intensity[2 * pair + c, n * OWN_BEAMS : (n + 1) * OWN_BEAMS, :] for c in range(2)], axis=0
                )
                outgoing[2 * n + to_core, pair * 16 : (pair + 1) * 16, :] = rows.astype(BF16)

    def shipment(distance, step, to_core):
        to = mate(distance, step, to_core)
        slot = (distance * GROUPS + step) * 2 + core
        return pltpu.make_async_remote_copy(
            src_ref=outgoing.at[to],
            dst_ref=incoming.at[slot],
            send_sem=send_sem,
            recv_sem=recv_sem.at[distance // 2],
            device_id=(to, freq_at),
            device_id_type=MESH,
        )

    def beams_and_send(to_core, carry):
        beams_of(to_core)

        @pl.when(to_core == 0)
        def _():
            pl.semaphore_wait(barrier, SENDERS - 1 + NEARS + FARS)

        for distance in range(GROUPS - 1, -1, -1):
            for step in range(GROUPS):
                if distance > 0 or step > 0:
                    shipment(distance, step, to_core).start()

        @pl.when(to_core != core)
        def _():
            shipment(0, 0, to_core).start()

        return carry

    lax.fori_loop(0, TURNS, beams_and_send, 0)
    keep = pltpu.make_async_copy(outgoing.at[beam_at], incoming.at[core], recv_sem.at[0])
    keep.start()

    lane = lax.broadcasted_iota(jnp.int32, (8, 128), 1)
    table_pad[...] = jnp.zeros_like(table_pad)
    table_pad[0:3, 0:ENTRIES] = merge_ref[...]
    code = table_pad[0:1, :] + 128 * table_pad[1:2, :] + 16384 * table_pad[2:3, :]
    pieces = [jnp.broadcast_to(code[:, 128 * n : 128 * (n + 1)], (8, 128)) for n in range(4)]
    turned = [pltpu.roll(piece, 32, 1) for piece in pieces]
    level_zero = pieces[0]
    level_one = pltpu.roll(pieces[0], 96, 1)
    level_two = jnp.where(lane < 32, turned[0], turned[1])
    last = [jnp.where(lane < 32, turned[1], turned[2]), jnp.where(lane < 32, turned[2], turned[3])]
    for part in range(2):
        subband = part * 8 + lax.broadcasted_iota(jnp.int32, (8, 128), 0)
        for half in range(2):
            found = last[half]
            late = jnp.zeros((8, 128), jnp.int32)
            for bit, level in ((3, level_two), (2, level_one), (1, level_zero), (0, None)):
                upper = lax.rem(jnp.right_shift(subband, bit), 2) == 1
                at = jnp.where(upper, jnp.right_shift(found, 7), found) & 127
                late = late + jnp.where(upper, jnp.right_shift(found, 14), 0)
                if level is not None:
                    found = jnp.take_along_axis(level, at, axis=1, mode="promise_in_bounds")
            table_vmem[pl.ds(part * 8, 8), pl.ds(half * 128, 128)] = at * 128 + late
    to_scalars = pltpu.make_async_copy(table_vmem, table, table_sem)
    to_scalars.start()

    channel = (
        ((row + GROUPS - jnp.right_shift(lane, 5)) & (GROUPS - 1)) * (GROUP * CHANNELS)
        + ((spot + GROUPS - (jnp.right_shift(lane, 3) & (GROUPS - 1))) & (GROUPS - 1)) * (2 * CHANNELS)
        + (jnp.right_shift(lane, 2) & 1) * CHANNELS
        + (lane & (CHANNELS - 1))
    )
    delays = jnp.concatenate(
        [
            jnp.take_along_axis(delay_ref[8 * n : 8 * n + 8, :], channel, axis=1, mode="promise_in_bounds")
            for n in range(TRIALS // 8)
        ],
        axis=0,
    )
    selector[...] = jnp.concatenate(
        [jnp.where(delays == n, 1.0, 0.0) for n in range(OFFSETS)], axis=0
    ).astype(BF16)

    half_way = SENDERS // 2

    def all_blocks(first, count):
        return pltpu.make_async_remote_copy(
            src_ref=outgoing.at[pl.ds(first, count)],
            dst_ref=incoming.at[pl.ds(first, count)],
            send_sem=send_sem,
            recv_sem=recv_sem.at[first // half_way],
            device_id=(lax.rem(beam_at + 1, SENDERS), freq_at),
            device_id_type=MESH,
        )

    block_rows = CHANNELS * OWN_BEAMS

    def spread_columns(first, last):
        rows_f32[first * block_rows : last * block_rows, :] = (
            incoming[first:last].astype(F32).reshape((last - first) * block_rows, SAMPLES)
        )
        for b in range(OWN_BEAMS):
            columns[first * CHANNELS : last * CHANNELS, b * SAMPLES : (b + 1) * SAMPLES] = rows_f32[
                pl.ds(first * block_rows + b, (last - first) * CHANNELS, stride=OWN_BEAMS), :
            ].astype(BF16)

    all_blocks(half_way, half_way).wait_recv()
    spread_columns(half_way, SENDERS)
    all_blocks(0, half_way).wait_recv()
    spread_columns(0, half_way)

    time = lax.broadcasted_iota(jnp.int32, (TRIALS, SAMPLES), 1)
    for pair in range(OWN_BEAMS // 2):
        spread = jnp.dot(
            selector[...], columns[:, pair * 2 * SAMPLES : (pair + 1) * 2 * SAMPLES], preferred_element_type=F32
        )
        for side in range(2):
            total = spread[:TRIALS, side * SAMPLES : (side + 1) * SAMPLES]
            for n in range(1, OFFSETS):
                piece = spread[n * TRIALS : (n + 1) * TRIALS, side * SAMPLES : (side + 1) * SAMPLES]
                total = total + jnp.where(time >= n, pltpu.roll(piece, n, 1), 0.0)
            b = 2 * pair + side
            partial_f32[b * TRIALS : (b + 1) * TRIALS, :] = total
    for r in range(TRIALS):
        window[0, r] = partial_f32[pl.ds(r, OWN_BEAMS, stride=TRIALS), :]
    own_block[...] = window[0].reshape(TRIALS * OWN_BEAMS, SAMPLES).astype(BF16)

    nears = []
    for slot, offset in enumerate(near_offsets):
        near = pltpu.make_async_remote_copy(
            src_ref=own_block,
            dst_ref=window_in.at[slot],
            send_sem=near_send.at[slot],
            recv_sem=near_recv.at[slot],
            device_id=(beam_at, ring(-offset)),
            device_id_type=MESH,
        )
        near.start()
        nears.append(near)

    def take_near(slot):
        nears[slot].wait_recv()
        window[slot + 1] = window_in[slot].astype(F32).reshape(TRIALS, OWN_BEAMS, SAMPLES)

    for slot in (2, 3, 0, 1):
        take_near(slot)

    to_scalars.wait()
    subbands = [freq_at] + [ring(offset) for offset in near_offsets]
    moment = lax.broadcasted_iota(jnp.int32, (OWN_BEAMS, SAMPLES), 1)

    def window_sum(to, k, places):
        total = None
        for place in range(places):
            entry = table[subbands[place], to * TRIALS + k]
            late = entry & 127
            moved = pltpu.roll(window[place, jnp.right_shift(entry, 7) & (TRIALS - 1)], late, 1)
            moved = jnp.where(moment >= late, moved, 0.0)
            total = moved if total is None else total + moved
        return total

    fars = []
    for slot, offset in enumerate(far_offsets):
        to = ring(-offset)

        def two_rows(n, carry, to=to, slot=slot):
            both = jnp.concatenate(
                [window_sum(to, 2 * n + side, PLACES - 1) for side in range(2)], axis=0
            )
            sums_out[slot, pl.ds(pl.multiple_of(n * 16, 16), 16), :] = both.astype(BF16)
            return carry

        lax.fori_loop(0, TRIALS // 2, two_rows, 0, unroll=4)
        far = pltpu.make_async_remote_copy(
            src_ref=sums_out.at[slot],
            dst_ref=sums_in.at[slot],
            send_sem=far_send.at[slot],
            recv_sem=far_recv.at[slot],
            device_id=(beam_at, to),
            device_id_type=MESH,
        )
        far.start()
        fars.append(far)

    take_near(NEARS - 1)

    def own_rows(k, carry):
        out_ref[k] = window_sum(freq_at, k, PLACES)
        return carry

    lax.fori_loop(0, TRIALS, own_rows, 0, unroll=8)

    all_blocks(0, SENDERS - 1).wait_send()
    for near in nears:
        near.wait_send()
    for far in fars:
        far.wait()
    gathered = sums_in[0].astype(F32) + sums_in[1].astype(F32)
    out_ref[...] = (out_ref[...] + gathered.reshape(TRIALS, OWN_BEAMS, SAMPLES)) * (1.0 / math.sqrt(2048.0))


def on_device(voltages, gains, channel_map, positions, directions, local_delay, merge_table):
    received = SENDERS * CHANNELS * OWN_BEAMS
    block = TRIALS * OWN_BEAMS
    return pl.pallas_call(
        kernel,
        out_shape=pltpu.VMEM((TRIALS, OWN_BEAMS, SAMPLES), F32),
        in_specs=[pl.BlockSpec(memory_space=pl.ANY)] * 7,
        out_specs=pl.BlockSpec(memory_space=pltpu.VMEM),
        scratch_shapes=[
            pltpu.VMEM((CHANNELS, 2, ANTENNAS), F32),
            pltpu.SMEM((CHANNELS,), jnp.int32),
            pltpu.VMEM((2, ANTENNAS), F32),
            pltpu.VMEM((2, BEAMS), F32),
            pltpu.VMEM((TRIALS, SENDERS * CHANNELS), jnp.int32),
            pltpu.VMEM((3, ENTRIES), jnp.int32),
            pltpu.VMEM((CHANNELS, ANTENNAS, 2 * SAMPLES), BF16),
            pltpu.VMEM((BEAMS, ANTENNAS), F32),
            pltpu.VMEM((2, BEAMS, 128), F32),
            pltpu.VMEM((CHANNELS, TURN_BEAMS, SAMPLES), F32),
            pltpu.VMEM((SENDERS, CHANNELS * OWN_BEAMS, SAMPLES), BF16),
            pltpu.VMEM((SENDERS, CHANNELS * OWN_BEAMS, SAMPLES), BF16),
            pltpu.VMEM((received + OWN_BEAMS, SAMPLES), F32),
            pltpu.VMEM((SENDERS * CHANNELS, OWN_BEAMS * SAMPLES), BF16),
            pltpu.VMEM((OFFSETS * TRIALS, SENDERS * CHANNELS), BF16),
            pltpu.VMEM((block + TRIALS, SAMPLES), F32),
            pltpu.VMEM((PLACES, TRIALS, OWN_BEAMS, SAMPLES), F32),
            pltpu.VMEM((block, SAMPLES), BF16),
            pltpu.VMEM((NEARS, block, SAMPLES), BF16),
            pltpu.VMEM((FARS, block, SAMPLES), BF16),
            pltpu.VMEM((FARS, block, SAMPLES), BF16),
            pltpu.VMEM((8, 512), jnp.int32),
            pltpu.VMEM((SUBBANDS, 256), jnp.int32),
            pltpu.SMEM((SUBBANDS, 256), jnp.int32),
            pltpu.SemaphoreType.DMA((6,)),
            pltpu.SemaphoreType.DMA((CHANNELS,)),
            pltpu.SemaphoreType.DMA,
            pltpu.SemaphoreType.DMA,
            pltpu.SemaphoreType.DMA((2,)),
            pltpu.SemaphoreType.DMA((NEARS,)),
            pltpu.SemaphoreType.DMA((NEARS,)),
            pltpu.SemaphoreType.DMA((FARS,)),
            pltpu.SemaphoreType.DMA((FARS,)),
        ],
        compiler_params=pltpu.CompilerParams(
            collective_id=0, has_side_effects=True, vmem_limit_bytes=48 * 2**20
        ),
        name="search_window",
    )(*[
        pltpu.with_memory_space_constraint(operand, pltpu.HBM)
        for operand in (voltages, gains, channel_map, positions, directions, local_delay, merge_table)
    ])


def solution(mesh):
    return jax.shard_map(
        on_device,
        mesh=mesh,
        in_specs=(
            P(("beam", "freq"), None, None),
            P(("beam", "freq"), None, None),
            P(("beam", "freq")),
            P(),
            P(),
            P("freq", None),
            P(),
        ),
        out_specs=P("freq", "beam", None),
        check_vma=False,
    )
```

profile of v0, /device:TPU:1, one launch (start us, length us, event | category | flops | bytes accessed | tf_op | source)
XLA Modules:
  0.0 35.0 jit_solution(6006409300487279340)
XLA Ops:
  0.0 34.4 %search_window.1 = f32[16,8,128]{2,1,0:T(8,128)S(1)} custom-call(bf16[4,1024,256]{2,1,0:T(8,128)(2,1)} %volts_hbm.1, f32[4,2,1024]{2,1,0:T(2,128)} %gains_hbm.1, s32[4]{0:T(128)} %channel_hbm.1, f32[2,1024]{1,0:T(2,128)} %positions_hbm.1, f32[2,256]{1,0:T(2,128)} %directions_hbm.1, s32[16,128]{1,0:T(8,128)} %delay_hbm.1, s32[3,480]{1,0:T(4,128)} %merge_hbm.1), custom_call_target="tpu_custom_call" | custom-call | tf_op jit(solution)/shard_map/search_window/pallas_call | solution.py:355
  34.4 0.6 %copy.9 = f32[16,8,128]{2,1,0:T(8,128)} copy(f32[16,8,128]{2,1,0:T(8,128)S(1)} %search_window.1) | data formatting | bytes 131072
where the time goes:
time: 35.4 us; the launch traced here: 35 us
  Pallas kernels  34.4 us (97%)
  local copies, waits for them, and re-layouts  0.63 us (2%)
    pallas_call x1, Pallas kernels, on_device(): pl.pallas_call(kernel, out_shape=pltpu.VMEM((TRIALS, OWN_BEAMS, SAMPLES),...  34.4 us

commit v1 on v0

--- a/solution.py
+++ b/solution.py
@@ -31,6 +31,11 @@
 NEARS = PLACES - 1
 FARS = 2
 ENTRIES = 480
+PART = 256
+ORDER = (
+    (2, 2), (1, 1), (3, 3), (0, 2), (2, 1), (1, 2), (3, 2), (0, 1),
+    (2, 3), (1, 3), (3, 1), (0, 3), (2, 0), (1, 0), (3, 0), (0, 0),
+)
 
 SIN_TERMS = (2.22143036, -0.91317465, 0.10983828)
 ROUNDER = 12582912.0
@@ -124,72 +129,152 @@
     for load in loads:
         load.wait()
 
-    half_width = ANTENNAS // 2
-
-    def beams_of(to_core):
-        for c in range(CHANNELS):
-            ratio = 1.0 + channel_ref[c].astype(F32) * (1.0 / 2048.0)
-            product = None
-            for half in range(2):
-                lanes = pl.ds(half * half_width, half_width)
-                gain_re = jnp.broadcast_to(gains_ref[c, 0:1, lanes] * (1.0 / 32.0), (16, half_width))
-                gain_im = jnp.broadcast_to(gains_ref[c, 1:2, lanes] * (1.0 / 32.0), (16, half_width))
-                real, imag = [], []
-                for n in range(TURN_BEAMS // 16):
-                    at = pl.ds(pl.multiple_of(to_core * (BEAMS // 2) + n * 16, 16), 16)
-                    pair = weight_pair(geometry[at, lanes], ratio, gain_re, gain_im)
-                    real.append(pair[0].astype(BF16))
-                    imag.append(pair[1].astype(BF16))
-                weights = jnp.concatenate(real + imag, axis=0)
-                term = jnp.dot(weights, volts[c, lanes, :], preferred_element_type=F32)
-                product = term if product is None else product + term
-            beam_re = product[:TURN_BEAMS, :SAMPLES] - product[TURN_BEAMS:, SAMPLES:]
-            beam_im = product[:TURN_BEAMS, SAMPLES:] + product[TURN_BEAMS:, :SAMPLES]
-            power = beam_re * beam_re + beam_im * beam_im
-            mean = jnp.sum(power, axis=1, keepdims=True) * (1.0 / SAMPLES)
-            intensity[c] = 0.25 * (power - mean)
-        for n in range(TURN_SENDS):
-            for pair in range(CHANNELS // 2):
-                rows = jnp.concatenate(
-                    [intensity[2 * pair + c, n * OWN_BEAMS : (n + 1) * OWN_BEAMS, :] for c in range(2)], axis=0
-                )
-                outgoing[2 * n + to_core, pair * 16 : (pair + 1) * 16, :] = rows.astype(BF16)
-
-    def shipment(distance, step, to_core):
+    def weights_of(to_core, c, part):
+        lanes = pl.ds(part * PART, PART)
+        ratio = 1.0 + channel_ref[c].astype(F32) * (1.0 / 2048.0)
+        gain_re = jnp.broadcast_to(gains_ref[c, 0:1, lanes] * (1.0 / 32.0), (16, PART))
+        gain_im = jnp.broadcast_to(gains_ref[c, 1:2, lanes] * (1.0 / 32.0), (16, PART))
+        real, imag = [], []
+        for n in range(TURN_BEAMS // 16):
+            at = pl.ds(pl.multiple_of(to_core * (BEAMS // 2) + n * 16, 16), 16)
+            pair = weight_pair(geometry[at, lanes], ratio, gain_re, gain_im)
+            real.append(pair[0].astype(BF16))
+            imag.append(pair[1].astype(BF16))
+        return jnp.concatenate(real + imag, axis=0)
+
+    def intensity_of(product):
+        beam_re = product[:TURN_BEAMS, :SAMPLES] - product[TURN_BEAMS:, SAMPLES:]
+        beam_im = product[:TURN_BEAMS, SAMPLES:] + product[TURN_BEAMS:, :SAMPLES]
+        power = beam_re * beam_re + beam_im * beam_im
+        mean = jnp.sum(power, axis=1, keepdims=True) * (1.0 / SAMPLES)
+        return 0.25 * (power - mean)
+
+    def shipment(distance, step, to_core, pair):
         to = mate(distance, step, to_core)
-        slot = (distance * GROUPS + step) * 2 + core
+        tile = pl.ds(pair * 16, 16)
         return pltpu.make_async_remote_copy(
-            src_ref=outgoing.at[to],
-            dst_ref=incoming.at[slot],
+            src_ref=outgoing.at[to, tile],
+            dst_ref=incoming.at[(distance * GROUPS + step) * 2 + core, tile],
             send_sem=send_sem,
             recv_sem=recv_sem.at[distance // 2],
             device_id=(to, freq_at),
             device_id_type=MESH,
         )
 
-    def beams_and_send(to_core, carry):
-        beams_of(to_core)
-
-        @pl.when(to_core == 0)
-        def _():
-            pl.semaphore_wait(barrier, SENDERS - 1 + NEARS + FARS)
-
-        for distance in range(GROUPS - 1, -1, -1):
-            for step in range(GROUPS):
-                if distance > 0 or step > 0:
-                    shipment(distance, step, to_core).start()
+    def send_pair(to_core, pair):
+        for n in range(TURN_SENDS):
+            at = slice(n * OWN_BEAMS, (n + 1) * OWN_BEAMS)
+            rows = jnp.concatenate([intensity[2 * pair + c, at, :] for c in range(2)], axis=0)
+            outgoing[2 * n + to_core, pair * 16 : (pair + 1) * 16, :] = rows.astype(BF16)
+        if pair == 0:
+
+            @pl.when(to_core == 0)
+            def _():
+                pl.semaphore_wait(barrier, SENDERS - 1 + NEARS + FARS)
+
+        for distance, step in ORDER[:-1]:
+            shipment(distance, step, to_core, pair).start()
 
         @pl.when(to_core != core)
         def _():
-            shipment(0, 0, to_core).start()
-
+            shipment(0, 0, to_core, pair).start()
+
+    def beams_of(to_core):
+        parts = [(c, part) for c in range(CHANNELS) for part in range(ANTENNAS // PART)]
+        ready, product = weights_of(to_core, *parts[0]), None
+        for n, (c, part) in enumerate(parts):
+            following = weights_of(to_core, *parts[n + 1]) if n + 1 < len(parts) else None
+            term = jnp.dot(ready, volts[c, pl.ds(part * PART, PART), :], preferred_element_type=F32)
+            product = term if part == 0 else product + term
+            if part + 1 == ANTENNAS // PART:
+                intensity[c] = intensity_of(product)
+                if c % 2 == 1:
+                    send_pair(to_core, c // 2)
+            ready = following
+
+    def one_turn(to_core, carry):
+        beams_of(to_core)
         return carry
 
-    lax.fori_loop(0, TURNS, beams_and_send, 0)
+    lax.fori_loop(0, TURNS, one_turn, 0)
     keep = pltpu.make_async_copy(outgoing.at[beam_at], incoming.at[core], recv_sem.at[0])
     keep.start()
 
     lane = lax.broadcasted_iota(jnp.int32, (8, 128), 1)
+    channel = (
+        ((row + GROUPS - jnp.right_shift(lane, 5)) & (GROUPS - 1)) * (GROUP * CHANNELS)
+        + ((spot + GROUPS - (jnp.right_shift(lane, 3) & (GROUPS - 1))) & (GROUPS - 1)) * (2 * CHANNELS)
+        + (jnp.right_shift(lane, 2) & 1) * CHANNELS
+        + (lane & (CHANNELS - 1))
+    )
+    delays = jnp.concatenate(
+        [
+            jnp.take_along_axis(delay_ref[8 * n : 8 * n + 8, :], channel, axis=1, mode="promise_in_bounds")
+            for n in range(TRIALS // 8)
+        ],
+        axis=0,
+    )
+    selector[...] = jnp.concatenate(
+        [jnp.where(delays == n, 1.0, 0.0) for n in range(OFFSETS)], axis=0
+    ).astype(BF16)
+
+    half_way = SENDERS // 2
+
+    def all_blocks(first, count):
+        return pltpu.make_async_remote_copy(
+            src_ref=outgoing.at[pl.ds(first, count)],
+            dst_ref=incoming.at[pl.ds(first, count)],
+            send_sem=send_sem,
+            recv_sem=recv_sem.at[first // half_way],
+            device_id=(lax.rem(beam_at + 1, SENDERS), freq_at),
+            device_id_type=MESH,
+        )
+
+    block_rows = CHANNELS * OWN_BEAMS
+
+    def spread_columns(first, last):
+        rows_f32[first * block_rows : last * block_rows, :] = (
+            incoming[first:last].astype(F32).reshape((last - first) * block_rows, SAMPLES)
+        )
+        for b in range(OWN_BEAMS):
+            columns[first * CHANNELS : last * CHANNELS, b * SAMPLES : (b + 1) * SAMPLES] = rows_f32[
+                pl.ds(first * block_rows + b, (last - first) * CHANNELS, stride=OWN_BEAMS), :
+            ].astype(BF16)
+
+    all_blocks(half_way, half_way).wait_recv()
+    spread_columns(half_way, SENDERS)
+    all_blocks(0, half_way).wait_recv()
+    spread_columns(0, half_way)
+
+    time = lax.broadcasted_iota(jnp.int32, (TRIALS, SAMPLES), 1)
+    for pair in range(OWN_BEAMS // 2):
+        spread = jnp.dot(
+            selector[...], columns[:, pair * 2 * SAMPLES : (pair + 1) * 2 * SAMPLES], preferred_element_type=F32
+        )
+        for side in range(2):
+            total = spread[:TRIALS, side * SAMPLES : (side + 1) * SAMPLES]
+            for n in range(1, OFFSETS):
+                piece = spread[n * TRIALS : (n + 1) * TRIALS, side * SAMPLES : (side + 1) * SAMPLES]
+                total = total + jnp.where(time >= n, pltpu.roll(piece, n, 1), 0.0)
+            b = 2 * pair + side
+            partial_f32[b * TRIALS : (b + 1) * TRIALS, :] = total
+    for r in range(TRIALS):
+        window[0, r] = partial_f32[pl.ds(r, OWN_BEAMS, stride=TRIALS), :]
+    own_block[...] = window[0].reshape(TRIALS * OWN_BEAMS, SAMPLES).astype(BF16)
+
+    nears = []
+    for slot, offset in enumerate(near_offsets):
+        near = pltpu.make_async_remote_copy(
+            src_ref=own_block,
+            dst_ref=window_in.at[slot],
+            send_sem=near_send.at[slot],
+            recv_sem=near_recv.at[slot],
+            device_id=(beam_at, ring(-offset)),
+            device_id_type=MESH,
+        )
+        near.start()
+        nears.append(near)
+
     table_pad[...] = jnp.zeros_like(table_pad)
     table_pad[0:3, 0:ENTRIES] = merge_ref[...]
     code = table_pad[0:1, :] + 128 * table_pad[1:2, :] + 16384 * table_pad[2:3, :]
@@ -213,80 +298,6 @@
             table_vmem[pl.ds(part * 8, 8), pl.ds(half * 128, 128)] = at * 128 + late
     to_scalars = pltpu.make_async_copy(table_vmem, table, table_sem)
     to_scalars.start()
-
-    channel = (
-        ((row + GROUPS - jnp.right_shift(lane, 5)) & (GROUPS - 1)) * (GROUP * CHANNELS)
-        + ((spot + GROUPS - (jnp.right_shift(lane, 3) & (GROUPS - 1))) & (GROUPS - 1)) * (2 * CHANNELS)
-        + (jnp.right_shift(lane, 2) & 1) * CHANNELS
-        + (lane & (CHANNELS - 1))
-    )
-    delays = jnp.concatenate(
-        [
-            jnp.take_along_axis(delay_ref[8 * n : 8 * n + 8, :], channel, axis=1, mode="promise_in_bounds")
-            for n in range(TRIALS // 8)
-        ],
-        axis=0,
-    )
-    selector[...] = jnp.concatenate(
-        [jnp.where(delays == n, 1.0, 0.0) for n in range(OFFSETS)], axis=0
-    ).astype(BF16)
-
-    half_way = SENDERS // 2
-
-    def all_blocks(first, count):
-        return pltpu.make_async_remote_copy(
-            src_ref=outgoing.at[pl.ds(first, count)],
-            dst_ref=incoming.at[pl.ds(first, count)],
-            send_sem=send_sem,
-            recv_sem=recv_sem.at[first // half_way],
-            device_id=(lax.rem(beam_at + 1, SENDERS), freq_at),
-            device_id_type=MESH,
-        )
-
-    block_rows = CHANNELS * OWN_BEAMS
-
-    def spread_columns(first, last):
-        rows_f32[first * block_rows : last * block_rows, :] = (
-            incoming[first:last].astype(F32).reshape((last - first) * block_rows, SAMPLES)
-        )
-        for b in range(OWN_BEAMS):
-            columns[first * CHANNELS : last * CHANNELS, b * SAMPLES : (b + 1) * SAMPLES] = rows_f32[
-                pl.ds(first * block_rows + b, (last - first) * CHANNELS, stride=OWN_BEAMS), :
-            ].astype(BF16)
-
-    all_blocks(half_way, half_way).wait_recv()
-    spread_columns(half_way, SENDERS)
-    all_blocks(0, half_way).wait_recv()
-    spread_columns(0, half_way)
-
-    time = lax.broadcasted_iota(jnp.int32, (TRIALS, SAMPLES), 1)
-    for pair in range(OWN_BEAMS // 2):
-        spread = jnp.dot(
-            selector[...], columns[:, pair * 2 * SAMPLES : (pair + 1) * 2 * SAMPLES], preferred_element_type=F32
-        )
-        for side in range(2):
-            total = spread[:TRIALS, side * SAMPLES : (side + 1) * SAMPLES]
-            for n in range(1, OFFSETS):
-                piece = spread[n * TRIALS : (n + 1) * TRIALS, side * SAMPLES : (side + 1) * SAMPLES]
-                total = total + jnp.where(time >= n, pltpu.roll(piece, n, 1), 0.0)
-            b = 2 * pair + side
-            partial_f32[b * TRIALS : (b + 1) * TRIALS, :] = total
-    for r in range(TRIALS):
-        window[0, r] = partial_f32[pl.ds(r, OWN_BEAMS, stride=TRIALS), :]
-    own_block[...] = window[0].reshape(TRIALS * OWN_BEAMS, SAMPLES).astype(BF16)
-
-    nears = []
-    for slot, offset in enumerate(near_offsets):
-        near = pltpu.make_async_remote_copy(
-            src_ref=own_block,
-            dst_ref=window_in.at[slot],
-            send_sem=near_send.at[slot],
-            recv_sem=near_recv.at[slot],
-            device_id=(beam_at, ring(-offset)),
-            device_id_type=MESH,
-        )
-        near.start()
-        nears.append(near)
 
     def take_near(slot):
         nears[slot].wait_recv()

time: 35.4 us -> 36.7 us (1.037)
  Pallas kernels: 34.4 us -> 35.9 us
    pallas_call x1, Pallas kernels: 34.4 us -> 35.9 us  [on_device(): pl.pallas_call(kernel, out_shape=pltpu.VMEM((TRIALS, OWN_BEAMS, SAMPLES),...]
where the time goes in v1:
time: 36.7 us; the launch traced here: 36.6 us
  Pallas kernels  35.9 us (98%)
  local copies, waits for them, and re-layouts  0.63 us (2%)
    pallas_call x1, Pallas kernels, on_device(): pl.pallas_call(kernel, out_shape=pltpu.VMEM((TRIALS, OWN_BEAMS, SAMPLES),...  35.9 us

profile of v1, /device:TPU:1, one launch (start us, length us, event | category | flops | bytes accessed | tf_op | source)
XLA Modules:
  0.0 36.6 jit_solution(5765821216575445458)
XLA Ops:
  0.0 35.9 %search_window.1 = f32[16,8,128]{2,1,0:T(8,128)S(1)} custom-call(bf16[4,1024,256]{2,1,0:T(8,128)(2,1)} %volts_hbm.1, f32[4,2,1024]{2,1,0:T(2,128)} %gains_hbm.1, s32[4]{0:T(128)} %channel_hbm.1, f32[2,1024]{1,0:T(2,128)} %positions_hbm.1, f32[2,256]{1,0:T(2,128)} %directions_hbm.1, s32[16,128]{1,0:T(8,128)} %delay_hbm.1, s32[3,480]{1,0:T(4,128)} %merge_hbm.1), custom_call_target="tpu_custom_call" | custom-call | tf_op jit(solution)/shard_map/search_window/pallas_call | solution.py:366
  36.0 0.6 %copy.9 = f32[16,8,128]{2,1,0:T(8,128)} copy(f32[16,8,128]{2,1,0:T(8,128)S(1)} %search_window.1) | data formatting | bytes 131072

commit v2 on v1

--- a/solution.py
+++ b/solution.py
@@ -66,7 +66,7 @@
 def kernel(
     volts_hbm, gains_hbm, channel_hbm, positions_hbm, directions_hbm, delay_hbm, merge_hbm, out_ref,
     gains_ref, channel_ref, positions_ref, directions_ref, delay_ref, merge_ref, volts, geometry, across, intensity, outgoing, incoming, rows_f32, columns,
-    selector, partial_f32, window, own_block, window_in, sums_out, sums_in, table_pad, table_vmem, table,
+    selector, partial_f32, window, own_block, window_in, sums_out, sums_in, early, table_pad, table_vmem, table,
     small_sem, volts_sem, table_sem, send_sem, recv_sem, near_send, near_recv, far_send, far_recv,
 ):
     beam_at = lax.axis_index("beam")
@@ -102,7 +102,7 @@
     for step in range(1, SENDERS):
         other = lax.rem(beam_at + step, SENDERS)
         pl.semaphore_signal(barrier, inc=1, device_id=(other, freq_at), device_id_type=MESH)
-    near_offsets = (-2, 2, -1, 1, 3 * lean)
+    near_offsets = (-1, 1, -2, 2, 3 * lean)
     far_offsets = (6 * lean, -5 * lean)
     for offset in near_offsets + far_offsets:
         pl.semaphore_signal(barrier, inc=1, device_id=(beam_at, ring(offset)), device_id_type=MESH)
@@ -149,36 +149,6 @@
         mean = jnp.sum(power, axis=1, keepdims=True) * (1.0 / SAMPLES)
         return 0.25 * (power - mean)
 
-    def shipment(distance, step, to_core, pair):
-        to = mate(distance, step, to_core)
-        tile = pl.ds(pair * 16, 16)
-        return pltpu.make_async_remote_copy(
-            src_ref=outgoing.at[to, tile],
-            dst_ref=incoming.at[(distance * GROUPS + step) * 2 + core, tile],
-            send_sem=send_sem,
-            recv_sem=recv_sem.at[distance // 2],
-            device_id=(to, freq_at),
-            device_id_type=MESH,
-        )
-
-    def send_pair(to_core, pair):
-        for n in range(TURN_SENDS):
-            at = slice(n * OWN_BEAMS, (n + 1) * OWN_BEAMS)
-            rows = jnp.concatenate([intensity[2 * pair + c, at, :] for c in range(2)], axis=0)
-            outgoing[2 * n + to_core, pair * 16 : (pair + 1) * 16, :] = rows.astype(BF16)
-        if pair == 0:
-
-            @pl.when(to_core == 0)
-            def _():
-                pl.semaphore_wait(barrier, SENDERS - 1 + NEARS + FARS)
-
-        for distance, step in ORDER[:-1]:
-            shipment(distance, step, to_core, pair).start()
-
-        @pl.when(to_core != core)
-        def _():
-            shipment(0, 0, to_core, pair).start()
-
     def beams_of(to_core):
         parts = [(c, part) for c in range(CHANNELS) for part in range(ANTENNAS // PART)]
         ready, product = weights_of(to_core, *parts[0]), None
@@ -188,15 +158,43 @@
             product = term if part == 0 else product + term
             if part + 1 == ANTENNAS // PART:
                 intensity[c] = intensity_of(product)
-                if c % 2 == 1:
-                    send_pair(to_core, c // 2)
             ready = following
-
-    def one_turn(to_core, carry):
+        for n in range(TURN_SENDS):
+            for pair in range(CHANNELS // 2):
+                rows = jnp.concatenate(
+                    [intensity[2 * pair + c, n * OWN_BEAMS : (n + 1) * OWN_BEAMS, :] for c in range(2)], axis=0
+                )
+                outgoing[2 * n + to_core, pair * 16 : (pair + 1) * 16, :] = rows.astype(BF16)
+
+    def shipment(distance, step, to_core):
+        to = mate(distance, step, to_core)
+        slot = (distance * GROUPS + step) * 2 + core
+        return pltpu.make_async_remote_copy(
+            src_ref=outgoing.at[to],
+            dst_ref=incoming.at[slot],
+            send_sem=send_sem,
+            recv_sem=recv_sem.at[distance // 2],
+            device_id=(to, freq_at),
+            device_id_type=MESH,
+        )
+
+    def beams_and_send(to_core, carry):
         beams_of(to_core)
+
+        @pl.when(to_core == 0)
+        def _():
+            pl.semaphore_wait(barrier, SENDERS - 1 + NEARS + FARS)
+
+        for distance, step in ORDER[:-1]:
+            shipment(distance, step, to_core).start()
+
+        @pl.when(to_core != core)
+        def _():
+            shipment(0, 0, to_core).start()
+
         return carry
 
-    lax.fori_loop(0, TURNS, one_turn, 0)
+    lax.fori_loop(0, TURNS, beams_and_send, 0)
     keep = pltpu.make_async_copy(outgoing.at[beam_at], incoming.at[core], recv_sem.at[0])
     keep.start()
 
@@ -303,16 +301,15 @@
         nears[slot].wait_recv()
         window[slot + 1] = window_in[slot].astype(F32).reshape(TRIALS, OWN_BEAMS, SAMPLES)
 
-    for slot in (2, 3, 0, 1):
-        take_near(slot)
-
     to_scalars.wait()
+    take_near(0)
+    take_near(1)
     subbands = [freq_at] + [ring(offset) for offset in near_offsets]
     moment = lax.broadcasted_iota(jnp.int32, (OWN_BEAMS, SAMPLES), 1)
 
     def window_sum(to, k, places):
         total = None
-        for place in range(places):
+        for place in places:
             entry = table[subbands[place], to * TRIALS + k]
             late = entry & 127
             moved = pltpu.roll(window[place, jnp.right_shift(entry, 7) & (TRIALS - 1)], late, 1)
@@ -320,24 +317,32 @@
             total = moved if total is None else total + moved
         return total
 
+    far_to = [ring(-offset) for offset in far_offsets]
+
+    def early_rows(k, carry):
+        for f in range(FARS):
+            early[f, k] = window_sum(far_to[f], k, (0, 1, 2))
+        return carry
+
+    lax.fori_loop(0, TRIALS, early_rows, 0, unroll=4)
+    take_near(2)
+    take_near(3)
+
     fars = []
-    for slot, offset in enumerate(far_offsets):
-        to = ring(-offset)
-
-        def two_rows(n, carry, to=to, slot=slot):
-            both = jnp.concatenate(
-                [window_sum(to, 2 * n + side, PLACES - 1) for side in range(2)], axis=0
-            )
-            sums_out[slot, pl.ds(pl.multiple_of(n * 16, 16), 16), :] = both.astype(BF16)
+    for f in range(FARS):
+
+        def two_rows(n, carry, f=f):
+            both = [early[f, k] + window_sum(far_to[f], k, (3, 4)) for k in (2 * n, 2 * n + 1)]
+            sums_out[f, pl.ds(pl.multiple_of(n * 16, 16), 16), :] = jnp.concatenate(both, axis=0).astype(BF16)
             return carry
 
-        lax.fori_loop(0, TRIALS // 2, two_rows, 0, unroll=4)
+        lax.fori_loop(0, TRIALS // 2, two_rows, 0, unroll=True)
         far = pltpu.make_async_remote_copy(
-            src_ref=sums_out.at[slot],
-            dst_ref=sums_in.at[slot],
-            send_sem=far_send.at[slot],
-            recv_sem=far_recv.at[slot],
-            device_id=(beam_at, to),
+            src_ref=sums_out.at[f],
+            dst_ref=sums_in.at[f],
+            send_sem=far_send.at[f],
+            recv_sem=far_recv.at[f],
+            device_id=(beam_at, far_to[f]),
             device_id_type=MESH,
         )
         far.start()
@@ -346,7 +351,7 @@
     take_near(NEARS - 1)
 
     def own_rows(k, carry):
-        out_ref[k] = window_sum(freq_at, k, PLACES)
+        out_ref[k] = window_sum(freq_at, k, range(PLACES))
         return carry
 
     lax.fori_loop(0, TRIALS, own_rows, 0, unroll=8)
@@ -390,6 +395,7 @@
             pltpu.VMEM((NEARS, block, SAMPLES), BF16),
             pltpu.VMEM((FARS, block, SAMPLES), BF16),
             pltpu.VMEM((FARS, block, SAMPLES), BF16),
+            pltpu.VMEM((FARS, TRIALS, OWN_BEAMS, SAMPLES), F32),
             pltpu.VMEM((8, 512), jnp.int32),
             pltpu.VMEM((SUBBANDS, 256), jnp.int32),
             pltpu.SMEM((SUBBANDS, 256), jnp.int32),

time: 36.7 us -> 36 us (0.981)
  Pallas kernels: 35.9 us -> 35.2 us
    pallas_call x1, Pallas kernels: 35.9 us -> 35.2 us  [on_device(): pl.pallas_call(kernel, out_shape=pltpu.VMEM((TRIALS, OWN_BEAMS, SAMPLES),...]
where the time goes in v2:
time: 36 us; the launch traced here: 35.9 us
  Pallas kernels  35.2 us (98%)
  local copies, waits for them, and re-layouts  0.63 us (2%)
    pallas_call x1, Pallas kernels, on_device(): pl.pallas_call(kernel, out_shape=pltpu.VMEM((TRIALS, OWN_BEAMS, SAMPLES),...  35.2 us

profile of v2, /device:TPU:1, one launch (start us, length us, event | category | flops | bytes accessed | tf_op | source)
XLA Modules:
  0.0 35.9 jit_solution(17644861656659171355)
XLA Ops:
  0.0 35.2 %search_window.1 = f32[16,8,128]{2,1,0:T(8,128)S(1)} custom-call(bf16[4,1024,256]{2,1,0:T(8,128)(2,1)} %volts_hbm.1, f32[4,2,1024]{2,1,0:T(2,128)} %gains_hbm.1, s32[4]{0:T(128)} %channel_hbm.1, f32[2,1024]{1,0:T(2,128)} %positions_hbm.1, f32[2,256]{1,0:T(2,128)} %directions_hbm.1, s32[16,128]{1,0:T(8,128)} %delay_hbm.1, s32[3,480]{1,0:T(4,128)} %merge_hbm.1), custom_call_target="tpu_custom_call" | custom-call | tf_op jit(solution)/shard_map/search_window/pallas_call | solution.py:371
  35.2 0.6 %copy.9 = f32[16,8,128]{2,1,0:T(8,128)} copy(f32[16,8,128]{2,1,0:T(8,128)S(1)} %search_window.1) | data formatting | bytes 131072

commit v3 on v2

--- a/solution.py
+++ b/solution.py
@@ -31,13 +31,14 @@
 NEARS = PLACES - 1
 FARS = 2
 ENTRIES = 480
-PART = 256
+PART = 512
 ORDER = (
-    (2, 2), (1, 1), (3, 3), (0, 2), (2, 1), (1, 2), (3, 2), (0, 1),
-    (2, 3), (1, 3), (3, 1), (0, 3), (2, 0), (1, 0), (3, 0), (0, 0),
+    (2, 2), (3, 3), (2, 1), (3, 2), (2, 3), (3, 1), (2, 0), (3, 0),
+    (1, 1), (0, 2), (1, 2), (0, 1), (1, 3), (0, 3), (1, 0), (0, 0),
 )
 
-SIN_TERMS = (2.22143036, -0.91317465, 0.10983828)
+SIN_TERMS = (2.641740790, -1.085953791, 0.130620464)
+ROOT_TWO = math.sqrt(2.0)
 ROUNDER = 12582912.0
 
 
@@ -54,12 +55,10 @@
     z = rest * rest
     quarter_sin = rest * horner(SIN_TERMS, z)
     square = quarter_sin * quarter_sin
-    left = 2.0 - square
+    left = 2.0 * ROOT_TWO - square
     half_sin = quarter_sin * (left * lax.rsqrt(left))
-    half_cos = 1.0 - square
-    doubled = half_sin + half_sin
-    cosine = 1.0 - doubled * half_sin
-    sine = doubled * half_cos
+    cosine = 1.0 - half_sin * half_sin
+    sine = half_sin * (ROOT_TWO - square)
     return gain_re * cosine + gain_im * sine, gain_im * cosine - gain_re * sine
 
 
@@ -85,17 +84,14 @@
     smalls = [
         pltpu.make_async_copy(src, dst, small_sem.at[n])
         for n, (src, dst) in enumerate((
-            (merge_hbm, merge_ref), (directions_hbm, directions_ref), (positions_hbm, positions_ref),
-            (gains_hbm, gains_ref), (channel_hbm, channel_ref), (delay_hbm, delay_ref),
+            (directions_hbm, directions_ref), (positions_hbm, positions_ref), (gains_hbm, gains_ref),
+            (channel_hbm, channel_ref), (delay_hbm, delay_ref), (merge_hbm, merge_ref),
         ))
     ]
     for small in smalls:
         small.start()
-    loads = [
-        pltpu.make_async_copy(volts_hbm.at[c], volts.at[c], volts_sem.at[c]) for c in range(CHANNELS)
-    ]
-    for load in loads:
-        load.start()
+    load = pltpu.make_async_copy(volts_hbm, volts, volts_sem)
+    load.start()
 
     barrier = pltpu.get_barrier_semaphore()
 
@@ -107,7 +103,7 @@
     for offset in near_offsets + far_offsets:
         pl.semaphore_signal(barrier, inc=1, device_id=(beam_at, ring(offset)), device_id_type=MESH)
 
-    for small in smalls:
+    for small in smalls[:2]:
         small.wait()
 
     for k in range(2):
@@ -126,8 +122,9 @@
         return carry
 
     lax.fori_loop(0, SENDERS // 2, geometry_rows, 0)
-    for load in loads:
-        load.wait()
+    for small in smalls[2:]:
+        small.wait()
+    load.wait()
 
     def weights_of(to_core, c, part):
         lanes = pl.ds(part * PART, PART)
@@ -400,7 +397,7 @@
             pltpu.VMEM((SUBBANDS, 256), jnp.int32),
             pltpu.SMEM((SUBBANDS, 256), jnp.int32),
             pltpu.SemaphoreType.DMA((6,)),
-            pltpu.SemaphoreType.DMA((CHANNELS,)),
+            pltpu.SemaphoreType.DMA,
             pltpu.SemaphoreType.DMA,
             pltpu.SemaphoreType.DMA,
             pltpu.SemaphoreType.DMA((2,)),

time: 36 us -> 36 us (level)
  no operation moved by 1% of the time
where the time goes in v3:
time: 36 us; the launch traced here: 35.8 us
  Pallas kernels  35.2 us (98%)
  local copies, waits for them, and re-layouts  0.63 us (2%)
    pallas_call x1, Pallas kernels, on_device(): pl.pallas_call(kernel, out_shape=pltpu.VMEM((TRIALS, OWN_BEAMS, SAMPLES),...  35.2 us

profile of v3, /device:TPU:1, one launch (start us, length us, event | category | flops | bytes accessed | tf_op | source)
XLA Modules:
  0.0 35.8 jit_solution(14951271953949437318)
XLA Ops:
  0.0 35.2 %search_window.1 = f32[16,8,128]{2,1,0:T(8,128)S(1)} custom-call(bf16[4,1024,256]{2,1,0:T(8,128)(2,1)} %volts_hbm.1, f32[4,2,1024]{2,1,0:T(2,128)} %gains_hbm.1, s32[4]{0:T(128)} %channel_hbm.1, f32[2,1024]{1,0:T(2,128)} %positions_hbm.1, f32[2,256]{1,0:T(2,128)} %directions_hbm.1, s32[16,128]{1,0:T(8,128)} %delay_hbm.1, s32[3,480]{1,0:T(4,128)} %merge_hbm.1), custom_call_target="tpu_custom_call" | custom-call | tf_op jit(solution)/shard_map/search_window/pallas_call | solution.py:368
  35.2 0.6 %copy.9 = f32[16,8,128]{2,1,0:T(8,128)} copy(f32[16,8,128]{2,1,0:T(8,128)S(1)} %search_window.1) | data formatting | bytes 131072

commit v4 on v3

--- a/solution.py
+++ b/solution.py
@@ -321,7 +321,7 @@
             early[f, k] = window_sum(far_to[f], k, (0, 1, 2))
         return carry
 
-    lax.fori_loop(0, TRIALS, early_rows, 0, unroll=4)
+    lax.fori_loop(0, TRIALS, early_rows, 0, unroll=8)
     take_near(2)
     take_near(3)
 

time: 36 us -> 34.9 us (0.969)
  Pallas kernels: 35.2 us -> 34.1 us
    pallas_call x1, Pallas kernels: 35.2 us -> 34.1 us  [on_device(): pl.pallas_call(kernel, out_shape=pltpu.VMEM((TRIALS, OWN_BEAMS, SAMPLES),...]
where the time goes in v4:
time: 34.9 us; the launch traced here: 34.7 us
  Pallas kernels  34.1 us (98%)
  local copies, waits for them, and re-layouts  0.63 us (2%)
    pallas_call x1, Pallas kernels, on_device(): pl.pallas_call(kernel, out_shape=pltpu.VMEM((TRIALS, OWN_BEAMS, SAMPLES),...  34.1 us

profile of v4, /device:TPU:1, one launch (start us, length us, event | category | flops | bytes accessed | tf_op | source)
XLA Modules:
  0.0 34.7 jit_solution(5271603950412442540)
XLA Ops:
  0.0 34.1 %search_window.1 = f32[16,8,128]{2,1,0:T(8,128)S(1)} custom-call(bf16[4,1024,256]{2,1,0:T(8,128)(2,1)} %volts_hbm.1, f32[4,2,1024]{2,1,0:T(2,128)} %gains_hbm.1, s32[4]{0:T(128)} %channel_hbm.1, f32[2,1024]{1,0:T(2,128)} %positions_hbm.1, f32[2,256]{1,0:T(2,128)} %directions_hbm.1, s32[16,128]{1,0:T(8,128)} %delay_hbm.1, s32[3,480]{1,0:T(4,128)} %merge_hbm.1), custom_call_target="tpu_custom_call" | custom-call | tf_op jit(solution)/shard_map/search_window/pallas_call | solution.py:368
  34.1 0.6 %copy.9 = f32[16,8,128]{2,1,0:T(8,128)} copy(f32[16,8,128]{2,1,0:T(8,128)S(1)} %search_window.1) | data formatting | bytes 131072

commit v5 on v4

--- a/solution.py
+++ b/solution.py
@@ -321,7 +321,7 @@
             early[f, k] = window_sum(far_to[f], k, (0, 1, 2))
         return carry
 
-    lax.fori_loop(0, TRIALS, early_rows, 0, unroll=8)
+    lax.fori_loop(0, TRIALS, early_rows, 0, unroll=16)
     take_near(2)
     take_near(3)
 

time: 34.9 us -> 34.9 us (level)
  no operation moved by 1% of the time
where the time goes in v5:
time: 34.9 us; the launch traced here: 34.7 us
  Pallas kernels  34.1 us (98%)
  local copies, waits for them, and re-layouts  0.63 us (2%)
    pallas_call x1, Pallas kernels, on_device(): pl.pallas_call(kernel, out_shape=pltpu.VMEM((TRIALS, OWN_BEAMS, SAMPLES),...  34.1 us

profile of v5, /device:TPU:1, one launch (start us, length us, event | category | flops | bytes accessed | tf_op | source)
XLA Modules:
  0.0 34.7 jit_solution(11805004364392291360)
XLA Ops:
  0.0 34.1 %search_window.1 = f32[16,8,128]{2,1,0:T(8,128)S(1)} custom-call(bf16[4,1024,256]{2,1,0:T(8,128)(2,1)} %volts_hbm.1, f32[4,2,1024]{2,1,0:T(2,128)} %gains_hbm.1, s32[4]{0:T(128)} %channel_hbm.1, f32[2,1024]{1,0:T(2,128)} %positions_hbm.1, f32[2,256]{1,0:T(2,128)} %directions_hbm.1, s32[16,128]{1,0:T(8,128)} %delay_hbm.1, s32[3,480]{1,0:T(4,128)} %merge_hbm.1), custom_call_target="tpu_custom_call" | custom-call | tf_op jit(solution)/shard_map/search_window/pallas_call | solution.py:368
  34.1 0.6 %copy.9 = f32[16,8,128]{2,1,0:T(8,128)} copy(f32[16,8,128]{2,1,0:T(8,128)S(1)} %search_window.1) | data formatting | bytes 131072
